TPU v7x, 128 devices: a whole 4x4x4 slice. The times are simulated.
128 devices in a mesh: sec: 4 (over x_hi, core), dev: 32 (over z, y, x_lo).
Axes of the slice: x: 4 (x_hi: 2, x_lo: 2; x = x_hi * 2 + x_lo), y: 4, z: 4, core: 2. Of those that a mesh axis runs over, the one named last changes fastest.
Arguments:
- queries: bfloat16 [1024, 64, 576], P(('sec', 'dev')), may hold values from -6 to 6
- latent_cache: bfloat16 [1024, 1024, 576], P(('sec', 'dev')), may hold values from -9 to 9
- cache_length: int32 [1024], P(('sec', 'dev')), may hold values from 2 to 1024, as said below
- residual: bfloat16 [1024, 7168], P(('sec', 'dev')), may hold values from -9 to 9
- norm_gain: float32 [7168], replicated, may hold values from 0.1 to 1.9
- value_up: bfloat16 [64, 512, 128], P('dev'), may hold values from -4 to 4
- out_weight: bfloat16 [8192, 7168], P('dev'), may hold values from -0.0625 to 0.0625
- gate_weight: bfloat16 [7168, 8192], P(None, 'dev'), may hold values from -0.0625 to 0.0625
- up_weight: bfloat16 [7168, 8192], P(None, 'dev'), may hold values from -0.0625 to 0.0625
- down_weight: bfloat16 [8192, 7168], P('dev'), may hold values from -0.125 to 0.125
- expert_index: int32 [1024, 2], P(('sec', 'dev')), may hold values from 0 to 3, all different within a row; in each aligned block of 4 rows (0 to 3, 4 to 7, ...) at most 3 rows name the same one
- gate_level: int32 [1024, 2], P(('sec', 'dev')), may hold values from 1 to 4095
Outputs:
- layer_output: bfloat16 [1024, 7168], P(('sec', 'dev'))
Inputs may be any that keep to these rules, and one draw needn't show every extreme that they name: `expert_index`: each token names 2 different experts. The rows of one device form 2 aligned blocks of 4 rows, and within such a block no expert is named more than 3 times. `cache_length`: some request of the first 3 sections holds exactly 1024 live positions.
All inputs are finite; a program needn't handle non-finite values.
Results may differ from a plain program's by a relative error of at most 0.03.
Values may be sent and summed in bfloat16 or wider, within the bound.
A program may use at most 192 MiB of HBM per device.

v0:
```python
import jax
import jax.numpy as jnp
from jax import lax
from jax.sharding import PartitionSpec as P

EXPERTS = 4
TOPK = 2
MICRO = 2
CAP = 3


def from_behind(x, axis, by):
    length = lax.axis_size(axis)
    pairs = [(i, i + by) for i in range(length) if 0 <= i + by < length]
    return lax.ppermute(x, axis, pairs)


def expert_block(expert_rows, gate_weight, up_weight, down_weight):
    gate_hidden = jnp.dot(expert_rows, gate_weight, preferred_element_type=jnp.float32)
    up_hidden = jnp.dot(expert_rows, up_weight, preferred_element_type=jnp.float32)
    activated = (jax.nn.silu(gate_hidden) * up_hidden).astype(jnp.bfloat16)
    return jnp.dot(activated, down_weight, preferred_element_type=jnp.float32).astype(jnp.bfloat16)


def layer_block(
    queries,
    latent_cache,
    cache_length,
    residual,
    norm_gain,
    value_up,
    out_weight,
    gate_weight,
    up_weight,
    down_weight,
    expert_index,
    gate_level,
    groups,
):
    sections = lax.axis_size("sec")
    group_size = lax.axis_size("dev")
    section_index = lax.axis_index("sec")
    attending = section_index < sections - 1
    token_count = queries.shape[0]
    latent_width = value_up.shape[1]
    score_scale = (value_up.shape[2] + queries.shape[2] - latent_width) ** (-0.5)
    width = residual.shape[1]
    scores = (
        jnp.einsum("thc,tpc->thp", queries, latent_cache, preferred_element_type=jnp.float32)
        * score_scale
    )
    position = lax.broadcasted_iota(jnp.int32, (1, 1, latent_cache.shape[1]), 2)
    usable = position < cache_length[:, None, None]
    masked = jnp.where(usable, scores, -1e30)
    highest = jnp.max(masked, axis=2, keepdims=True)
    expos = jnp.where(usable, jnp.exp(masked - highest), 0.0)
    weights = (expos / jnp.sum(expos, axis=2, keepdims=True)).astype(jnp.bfloat16)
    latent_out = jnp.einsum(
        "thp,tpc->thc", weights, latent_cache, preferred_element_type=jnp.float32
    )[:, :, :latent_width].astype(jnp.bfloat16)
    by_heads = lax.all_to_all(latent_out, "dev", split_axis=1, concat_axis=0, tiled=True)
    head_out = jnp.einsum(
        "thc,hcv->thv", by_heads, value_up, preferred_element_type=jnp.float32
    ).astype(jnp.bfloat16)
    head_flat = head_out.reshape(head_out.shape[0], -1)
    attended = lax.psum_scatter(
        jnp.dot(head_flat, out_weight, preferred_element_type=jnp.float32).astype(jnp.bfloat16),
        "dev",
        scatter_dimension=0,
        tiled=True,
    ).astype(jnp.float32)
    stream = (residual.astype(jnp.float32) + attended).astype(jnp.bfloat16)
    stream_float = stream.astype(jnp.float32)
    mean_square = jnp.mean(stream_float * stream_float, axis=1, keepdims=True)
    normed = (stream_float * lax.rsqrt(mean_square + 1e-06) * norm_gain).astype(jnp.bfloat16)
    route_count = token_count * TOPK
    per_micro = token_count // groups
    slot_width = groups * CAP
    flat_expert = expert_index.reshape(route_count)
    route_order = jnp.arange(route_count, dtype=jnp.int32)
    micro_of = route_order // TOPK // per_micro
    earlier = (
        (route_order[:, None] > route_order[None, :])
        & (flat_expert[:, None] == flat_expert[None, :])
        & (micro_of[:, None] == micro_of[None, :])
    )
    rank_in = jnp.sum(earlier.astype(jnp.int32), axis=1)
    target = (flat_expert * slot_width + micro_of * CAP + rank_in).reshape(token_count, TOPK)
    slot_index = jnp.arange(EXPERTS * slot_width, dtype=jnp.int32)
    placing = jnp.any(slot_index[:, None, None] == target[None, :, :], axis=2).astype(jnp.bfloat16)
    levels = gate_level.astype(jnp.float32)
    mix = levels / jnp.sum(levels, axis=1, keepdims=True)
    gathering = jnp.sum(
        jnp.where(slot_index[None, None, :] == target[:, :, None], mix[:, :, None], 0.0), axis=1
    )
    packed = jnp.dot(placing, normed, preferred_element_type=jnp.float32)
    packed = jnp.where(attending, packed, 0.0).astype(jnp.bfloat16)
    slab_count = group_size // EXPERTS
    last_section = sections - 1
    pieces = []
    for source in range(last_section):
        pieces.append(from_behind(packed, "sec", last_section - source))
    stacked = jnp.stack(pieces, axis=0).reshape(last_section, EXPERTS, 1, slot_width, width)
    spread = jnp.broadcast_to(stacked, (last_section, EXPERTS, slab_count, slot_width, width))
    spread = jnp.transpose(spread, (1, 2, 0, 3, 4)).reshape(
        group_size, last_section, slot_width, width
    )
    arrived = lax.all_to_all(spread, "dev", split_axis=0, concat_axis=0, tiled=True)
    partial_out = expert_block(arrived.reshape(-1, width), gate_weight, up_weight, down_weight)
    back = lax.all_to_all(
        partial_out.reshape(group_size, last_section, slot_width, width),
        "dev",
        split_axis=0,
        concat_axis=0,
        tiled=True,
    )
    from_flat = jnp.zeros((group_size, slot_width, width), jnp.bfloat16)
    for source in range(last_section):
        moved = from_behind(back[:, source], "sec", source - last_section)
        from_flat = jnp.where(section_index == source, moved, from_flat)
    from_experts = from_flat.reshape(EXPERTS, slab_count, slot_width, width)
    slab_total = jnp.sum(from_experts.astype(jnp.float32), axis=1).reshape(
        EXPERTS * slot_width, width
    )
    moe = jnp.dot(gathering, slab_total, precision=lax.Precision.HIGHEST)
    result = (stream_float + moe).astype(jnp.bfloat16)
    return jnp.where(attending, result, jnp.zeros_like(result))


def body(
    queries,
    latent_cache,
    cache_length,
    residual,
    norm_gain,
    value_up,
    out_weight,
    gate_weight,
    up_weight,
    down_weight,
    expert_index,
    gate_level,
):
    return layer_block(
        queries,
        latent_cache,
        cache_length,
        residual,
        norm_gain,
        value_up,
        out_weight,
        gate_weight,
        up_weight,
        down_weight,
        expert_index,
        gate_level,
        MICRO,
    )


def solution(mesh):
    placed = (
        P(("sec", "dev"), None, None),
        P(("sec", "dev"), None, None),
        P(("sec", "dev")),
        P(("sec", "dev"), None),
        P(),
        P("dev", None, None),
        P("dev", None),
        P(None, "dev"),
        P(None, "dev"),
        P("dev", None),
        P(("sec", "dev"), None),
        P(("sec", "dev"), None),
    )
    return jax.shard_map(
        body, mesh=mesh, in_specs=placed, out_specs=P(("sec", "dev"), None), check_vma=False
    )
```

profile of v0, /device:TPU:0, one launch (start us, length us, event | category | flops | bytes accessed | tf_op | source)
XLA Modules:
  0.0 691.1 jit_solution(9540365093698168124)
XLA Ops:
  7.6 6.0 fusion.32
  13.6 6.6 fusion.6
  20.6 21.5 %all_to_all.28 = bf16[8,64,512]{2,0,1:T(8,128)(2,1)S(1)} all-to-all(bf16[8,64,512]{2,0,1:T(8,128)(2,1)S(1)} %copy.49), channel_id=1, replica_groups=mesh['sec'=4,'dev'=32] {'dev'}, dimensions={1} | all-to-all | bytes 1048576 | tf_op jit(solution)/shard_map/all_to_all | solution.py:61
  42.5 2.9 convolution_convert_fusion.1
  46.8 168.3 %reduce-scatter.2.cloned.1.call-done = bf16[8,7168]{1,0:T(8,128)(2,1)} async-done(((bf16[256,7168]{1,0:T(8,128)(2,1)}), bf16[8,7168]{1,0:T(8,128)(2,1)}) %reduce-scatter.2.cloned.1.call-update) | async-done | bytes 114704 | tf_op jit(solution)/shard_map/reduce_scatter | solution.py:66
  217.4 1.3 collective-permute-start
  218.7 3.6 collective-permute-start.1
  223.8 6.3 collective-permute-done.1
  230.8 5.4 broadcast_in_dim.67
  236.2 132.8 %all_to_all.29 = bf16[32,3,6,7168]{3,2,1,0:T(8,128)(2,1)} all-to-all(bf16[32,3,6,7168]{3,2,1,0:T(8,128)(2,1)} %bitcast.46), channel_id=1, replica_groups=mesh['sec'=4,'dev'=32] {'dev'}, dimensions={0} | all-to-all | bytes 16515072 | tf_op jit(solution)/shard_map/all_to_all | solution.py:108
  369.0 12.5 %reshape.218 = bf16[576,7168]{1,0:T(8,128)(2,1)} reshape(bf16[32,3,6,7168]{3,2,1,0:T(8,128)(2,1)} %all_to_all.29) | data formatting | bytes 16515072 | tf_op jit(solution)/shard_map/reshape | solution.py:109
  381.5 6.7 fusion.35
  388.2 17.4 %convolution_convert_fusion = bf16[576,7168]{1,0:T(8,128)(2,1)} fusion(bf16[256,7168]{1,0:T(8,128)(2,1)} %param.21, bf16[576,7168]{1,0:T(8,128)(2,1)} %reshape.218, bf16[7168,256]{1,0:T(8,128)(2,1)} %param.20, f32[576,256]{1,0:T(8,128)S(1)} %fusion.35), kind=kOutput, calls=%fused_computation.1 | convolution fusion | flops 4232871936 | bytes 24444928 | tf_op jit(solution)/shard_map/dot_general | solution.py:22
  405.6 11.6 %reshape.219 = bf16[32,3,6,7168]{3,2,1,0:T(8,128)(2,1)} reshape(bf16[576,7168]{1,0:T(8,128)(2,1)} %convolution_convert_fusion) | data formatting | bytes 16515072 | tf_op jit(solution)/shard_map/reshape | solution.py:111
  417.2 132.9 %all_to_all.30 = bf16[32,3,6,7168]{3,2,1,0:T(8,128)(2,1)S(1)} all-to-all(bf16[32,3,6,7168]{3,2,1,0:T(8,128)(2,1)} %reshape.219), channel_id=1, replica_groups=mesh['sec'=4,'dev'=32] {'dev'}, dimensions={0} | all-to-all | bytes 16515072 | tf_op jit(solution)/shard_map/all_to_all | solution.py:110
  551.1 3.1 copy.57
  554.2 1.5 collective-permute-start.3
  555.7 3.1 copy.58
  558.7 1.4 collective-permute-start.4
  560.1 3.2 copy.59
  564.7 105.6 %collective-permute-done.4 = bf16[32,6,7168]{2,0,1:T(8,128)(2,1)} collective-permute-done((bf16[32,6,7168]{2,0,1:T(8,128)(2,1)}, bf16[32,6,7168]{2,0,1:T(8,128)(2,1)}, u32[]{:S(2)}, u32[]{:S(2)}) %collective-permute-start.4) | collective-permute-done | bytes 2752544 | tf_op jit(solution)/shard_map/ppermute | solution.py:15
  670.3 7.0 %collective-permute-done.5 = bf16[32,6,7168]{2,0,1:T(8,128)(2,1)} collective-permute-done((bf16[32,6,7168]{2,0,1:T(8,128)(2,1)}, bf16[32,6,7168]{2,0,1:T(8,128)(2,1)}, u32[]{:S(2)}, u32[]{:S(2)}) %collective-permute-start.5) | collective-permute-done | bytes 2752544 | tf_op jit(solution)/shard_map/ppermute | solution.py:15
  677.3 4.4 convert_reduce_fusion
  682.3 2.0 fusion.3
  (49 shorter events, 10.3 us)
Async XLA Ops:
  6.5 1.1 copy-start
  6.5 208.6 %reduce-scatter.2.cloned.1.call-start = ((), (), s32[]{:S(2)}) async-start(), calls=%async_computation.4 | async-start | bytes 3784704 | tf_op jit(solution)/shard_map/reduce_scatter | solution.py:66
  13.6 28.6 %copy-start.7 = (bf16[2,512,128]{2,1,0:T(8,128)(2,1)S(1)}, bf16[2,512,128]{2,1,0:T(8,128)(2,1)}, u32[]{:S(2)}) copy-start(bf16[2,512,128]{2,1,0:T(8,128)(2,1)} %param.17) | copy-start | bytes 786436
  20.3 22.2 %copy-start.2 = (bf16[256,7168]{1,0:T(8,128)(2,1)S(1)}, bf16[256,7168]{1,0:T(8,128)(2,1)}, u32[]{:S(2)}) copy-start(bf16[256,7168]{1,0:T(8,128)(2,1)} %param.18) | copy-start | bytes 11010052
  45.5 0.7 copy-start.5
  45.5 169.6 %copy-start.3 = (bf16[8,7168]{1,0:T(8,128)(2,1)S(1)}, bf16[8,7168]{1,0:T(8,128)(2,1)}, u32[]{:S(2)}) copy-start(bf16[8,7168]{1,0:T(8,128)(2,1)} %param.15) | copy-start | bytes 344068
  45.5 170.7 %copy-start.4 = (f32[7168]{0:T(1024)S(1)}, f32[7168]{0:T(1024)}, u32[]{:S(2)}) copy-start(f32[7168]{0:T(1024)} %param.16) | copy-start | bytes 86020
  217.4 6.3 collective-permute-start
  218.7 11.4 %collective-permute-start.1 = (bf16[24,7168]{1,0:T(8,128)(2,1)S(1)}, bf16[24,7168]{1,0:T(8,128)(2,1)S(1)}, u32[]{:S(2)}, u32[]{:S(2)}) collective-permute-start(bf16[24,7168]{1,0:T(8,128)(2,1)S(1)} %fusion.1), channel_id=1, source_target_pairs={{0,64},{32,96},{1,65},{33,97},{2,66},{34,98},{3,67},{35,99},{4,68}... | collective-permute-start | bytes 1032200 | tf_op jit(solution)/shard_map/ppermute | solution.py:15
  222.3 7.9 %collective-permute-start.2 = (bf16[24,7168]{1,0:T(8,128)(2,1)S(1)}, bf16[24,7168]{1,0:T(8,128)(2,1)S(1)}, u32[]{:S(2)}, u32[]{:S(2)}) collective-permute-start(bf16[24,7168]{1,0:T(8,128)(2,1)S(1)} %fusion.1), channel_id=1, source_target_pairs={{0,32},{32,64},{64,96},{1,33},{33,65},{65,97},{2,34},{34,66},{66,9... | collective-permute-start | bytes 1032200 | tf_op jit(solution)/shard_map/ppermute | solution.py:15
  554.2 10.6 %collective-permute-start.3 = (bf16[32,6,7168]{2,0,1:T(8,128)(2,1)}, bf16[32,6,7168]{2,0,1:T(8,128)(2,1)S(1)}, u32[]{:S(2)}, u32[]{:S(2)}) collective-permute-start(bf16[32,6,7168]{2,0,1:T(8,128)(2,1)} %copy.57), channel_id=1, source_target_pairs={{32,0},{64,32},{96,64},{33,1},{65,33},{97,65},{34,2},{66,34},{98,6... | collective-permute-start | bytes 8257544 | tf_op jit(solution)/shard_map/ppermute | solution.py:15
  558.7 5.9 copy-start.6
  558.7 111.6 %collective-permute-start.4 = (bf16[32,6,7168]{2,0,1:T(8,128)(2,1)}, bf16[32,6,7168]{2,0,1:T(8,128)(2,1)}, u32[]{:S(2)}, u32[]{:S(2)}) collective-permute-start(bf16[32,6,7168]{2,0,1:T(8,128)(2,1)} %copy.58), channel_id=1, source_target_pairs={{64,0},{96,32},{65,1},{97,33},{66,2},{98,34},{67,3},{99,35},{68,4}... | collective-permute-start | bytes 8257544 | tf_op jit(solution)/shard_map/ppermute | solution.py:15
  563.3 114.0 %collective-permute-start.5 = (bf16[32,6,7168]{2,0,1:T(8,128)(2,1)}, bf16[32,6,7168]{2,0,1:T(8,128)(2,1)}, u32[]{:S(2)}, u32[]{:S(2)}) collective-permute-start(bf16[32,6,7168]{2,0,1:T(8,128)(2,1)} %copy.59), channel_id=1, source_target_pairs={{96,0},{97,1},{98,2},{99,3},{100,4},{101,5},{102,6},{103,7},{104,8... | collective-permute-start | bytes 8257544 | tf_op jit(solution)/shard_map/ppermute | solution.py:15
  677.3 7.0 %copy-start.1 = (bf16[8,64,576]{2,1,0:T(8,128)(2,1)S(1)}, bf16[8,64,576]{2,1,0:T(8,128)(2,1)}, u32[]{:S(2)}) copy-start(bf16[8,64,576]{2,1,0:T(8,128)(2,1)} %param.12) | copy-start | bytes 1769476
Sparse Core Ops, SparseCore 0:
  45.6 169.4 reduce-scatter.1
where the time goes:
time: 692 us; the launch traced here: 691 us
  blocking collectives  287 us (41%)
  waiting for transfers between devices  287 us (41%)
  matrix products  43.2 us (6%)
  local copies, waits for them, and re-layouts  42.3 us (6%)
  between operations  13.6 us (2%)
  starting transfers between devices  10.4 us (2%)
  other arithmetic  7.04 us (1%)
    reduce_scatter x1, waiting for transfers between devices, layer_block(): lax.psum_scatter(jnp.dot(head_flat, out_weight, preferred_element_type=jn...  168 us
    all_to_all x1, blocking collectives, layer_block(): lax.all_to_all(partial_out.reshape(group_size, last_section, slot_width,...  133 us
    all_to_all x1, blocking collectives, layer_block(): lax.all_to_all(spread, 'dev', split_axis=0, concat_axis=0, tiled=True)  133 us
    ppermute x6, waiting for transfers between devices, from_behind(): return lax.ppermute(x, axis, pairs)  119 us
    all_to_all x1, blocking collectives, layer_block(): lax.all_to_all(latent_out, 'dev', split_axis=1, concat_axis=0, tiled=True)  21.5 us
    dot_general x1, matrix products, expert_block(): jnp.dot(activated, down_weight, preferred_element_type=jnp.float32)  17.4 us
  transfers between devices with their start and end apart: 7, of which 4 were waited for; matrix products, arithmetic and copies ran while one was open for 1% of the time, Pallas kernels for 0%

commit v1 on v0

--- a/solution.py
+++ b/solution.py
@@ -58,7 +58,10 @@
     latent_out = jnp.einsum(
         "thp,tpc->thc", weights, latent_cache, preferred_element_type=jnp.float32
     )[:, :, :latent_width].astype(jnp.bfloat16)
-    by_heads = lax.all_to_all(latent_out, "dev", split_axis=1, concat_axis=0, tiled=True)
+    by_heads = jnp.concatenate(
+        lax.all_to_all(jnp.stack(jnp.split(latent_out, lax.axis_size("dev"), axis=1)), "dev", 0, 0),
+        axis=0,
+    )
     head_out = jnp.einsum(
         "thc,hcv->thv", by_heads, value_up, preferred_element_type=jnp.float32
     ).astype(jnp.bfloat16)

time: 692 us -> 692 us (level)
  no operation moved by 1% of the time
where the time goes in v1:
time: 692 us; the launch traced here: 691 us
  blocking collectives  287 us (41%)
  waiting for transfers between devices  287 us (41%)
  matrix products  43.3 us (6%)
  local copies, waits for them, and re-layouts  42.9 us (6%)
  between operations  13.7 us (2%)
  starting transfers between devices  10.6 us (2%)
  other arithmetic  7.04 us (1%)
    reduce_scatter x1, waiting for transfers between devices, layer_block(): lax.psum_scatter(jnp.dot(head_flat, out_weight, preferred_element_type=jn...  168 us
    all_to_all x1, blocking collectives, layer_block(): lax.all_to_all(partial_out.reshape(group_size, last_section, slot_width,...  133 us
    all_to_all x1, blocking collectives, layer_block(): lax.all_to_all(spread, 'dev', split_axis=0, concat_axis=0, tiled=True)  132 us
    ppermute x6, waiting for transfers between devices, from_behind(): return lax.ppermute(x, axis, pairs)  119 us
    all_to_all x1, blocking collectives, layer_block(): lax.all_to_all(jnp.stack(jnp.split(latent_out, lax.axis_size('dev'), axis...  21.4 us
    dot_general x1, matrix products, expert_block(): jnp.dot(activated, down_weight, preferred_element_type=jnp.float32)  17.4 us
  transfers between devices with their start and end apart: 7, of which 4 were waited for; matrix products, arithmetic and copies ran while one was open for 1% of the time, Pallas kernels for 0%

profile of v1, /device:TPU:0, one launch (start us, length us, event | category | flops | bytes accessed | tf_op | source)
XLA Modules:
  0.0 691.2 jit_solution(14177672631491637753)
XLA Ops:
  7.6 6.0 fusion.30
  13.7 6.7 convolution_convert_fusion.2
  21.4 21.4 %all_to_all.15 = bf16[32,8,2,512]{3,2,1,0:T(2,128)(2,1)S(1)} all-to-all(bf16[32,8,2,512]{3,2,1,0:T(2,128)(2,1)S(1)} %constant_dynamic-update-slice_fusion), channel_id=1, replica_groups=mesh['sec'=4,'dev'=32] {'dev'}, dimensions={0} | all-to-all | bytes 1048576 | tf_op jit(solution)/shard_map/all_to_all | solution.py:62
  43.1 2.9 convolution_convert_fusion.1
  47.4 168.3 %reduce-scatter.2.cloned.1.call-done = bf16[8,7168]{1,0:T(8,128)(2,1)} async-done(((bf16[256,7168]{1,0:T(8,128)(2,1)}), bf16[8,7168]{1,0:T(8,128)(2,1)}) %reduce-scatter.2.cloned.1.call-update) | async-done | bytes 114704 | tf_op jit(solution)/shard_map/reduce_scatter | solution.py:69
  218.0 1.3 collective-permute-start
  219.3 3.8 collective-permute-start.1
  224.5 6.3 collective-permute-done.1
  231.5 5.4 broadcast_in_dim.67
  236.9 132.3 %all_to_all.16 = bf16[32,3,6,7168]{3,2,1,0:T(8,128)(2,1)} all-to-all(bf16[32,3,6,7168]{3,2,1,0:T(8,128)(2,1)} %bitcast.169), channel_id=1, replica_groups=mesh['sec'=4,'dev'=32] {'dev'}, dimensions={0} | all-to-all | bytes 16515072 | tf_op jit(solution)/shard_map/all_to_all | solution.py:111
  369.3 12.5 %reshape.222 = bf16[576,7168]{1,0:T(8,128)(2,1)} reshape(bf16[32,3,6,7168]{3,2,1,0:T(8,128)(2,1)} %all_to_all.16) | data formatting | bytes 16515072 | tf_op jit(solution)/shard_map/reshape | solution.py:112
  381.7 6.7 fusion.33
  388.4 17.4 %convolution_convert_fusion = bf16[576,7168]{1,0:T(8,128)(2,1)} fusion(bf16[256,7168]{1,0:T(8,128)(2,1)} %param.21, bf16[576,7168]{1,0:T(8,128)(2,1)} %reshape.222, bf16[7168,256]{1,0:T(8,128)(2,1)} %param.20, f32[576,256]{1,0:T(8,128)S(1)} %fusion.33), kind=kOutput, calls=%fused_computation.1 | convolution fusion | flops 4232871936 | bytes 24444928 | tf_op jit(solution)/shard_map/dot_general | solution.py:22
  405.8 11.6 %reshape.223 = bf16[32,3,6,7168]{3,2,1,0:T(8,128)(2,1)} reshape(bf16[576,7168]{1,0:T(8,128)(2,1)} %convolution_convert_fusion) | data formatting | bytes 16515072 | tf_op jit(solution)/shard_map/reshape | solution.py:114
  417.4 132.8 %all_to_all.17 = bf16[32,3,6,7168]{3,2,1,0:T(8,128)(2,1)S(1)} all-to-all(bf16[32,3,6,7168]{3,2,1,0:T(8,128)(2,1)} %reshape.223), channel_id=1, replica_groups=mesh['sec'=4,'dev'=32] {'dev'}, dimensions={0} | all-to-all | bytes 16515072 | tf_op jit(solution)/shard_map/all_to_all | solution.py:113
  551.2 3.1 copy.54
  554.2 1.5 collective-permute-start.3
  555.8 3.1 copy.55
  558.8 1.4 collective-permute-start.4
  560.2 3.2 copy.56
  564.8 105.5 %collective-permute-done.4 = bf16[32,6,7168]{2,0,1:T(8,128)(2,1)} collective-permute-done((bf16[32,6,7168]{2,0,1:T(8,128)(2,1)}, bf16[32,6,7168]{2,0,1:T(8,128)(2,1)}, u32[]{:S(2)}, u32[]{:S(2)}) %collective-permute-start.4) | collective-permute-done | bytes 2752544 | tf_op jit(solution)/shard_map/ppermute | solution.py:15
  670.3 7.1 %collective-permute-done.5 = bf16[32,6,7168]{2,0,1:T(8,128)(2,1)} collective-permute-done((bf16[32,6,7168]{2,0,1:T(8,128)(2,1)}, bf16[32,6,7168]{2,0,1:T(8,128)(2,1)}, u32[]{:S(2)}, u32[]{:S(2)}) %collective-permute-start.5) | collective-permute-done | bytes 2752544 | tf_op jit(solution)/shard_map/ppermute | solution.py:15
  677.4 4.4 convert_reduce_fusion
  682.3 2.0 fusion.3
  (79 shorter events, 10.8 us)
Async XLA Ops:
  6.5 1.1 copy-start
  6.5 209.1 %reduce-scatter.2.cloned.1.call-start = ((), (), s32[]{:S(2)}) async-start(), calls=%async_computation.4 | async-start | bytes 3784704 | tf_op jit(solution)/shard_map/reduce_scatter | solution.py:69
  13.6 29.2 %copy-start.7 = (bf16[2,512,128]{2,1,0:T(8,128)(2,1)S(1)}, bf16[2,512,128]{2,1,0:T(8,128)(2,1)}, u32[]{:S(2)}) copy-start(bf16[2,512,128]{2,1,0:T(8,128)(2,1)} %param.17) | copy-start | bytes 786436
  13.6 29.5 %copy-start.2 = (bf16[256,7168]{1,0:T(8,128)(2,1)S(1)}, bf16[256,7168]{1,0:T(8,128)(2,1)}, u32[]{:S(2)}) copy-start(bf16[256,7168]{1,0:T(8,128)(2,1)} %param.18) | copy-start | bytes 11010052
  46.1 0.7 copy-start.5
  46.1 169.6 %copy-start.3 = (bf16[8,7168]{1,0:T(8,128)(2,1)S(1)}, bf16[8,7168]{1,0:T(8,128)(2,1)}, u32[]{:S(2)}) copy-start(bf16[8,7168]{1,0:T(8,128)(2,1)} %param.15) | copy-start | bytes 344068
  46.1 170.7 %copy-start.4 = (f32[7168]{0:T(1024)S(1)}, f32[7168]{0:T(1024)}, u32[]{:S(2)}) copy-start(f32[7168]{0:T(1024)} %param.16) | copy-start | bytes 86020
  218.0 6.4 collective-permute-start
  219.3 11.5 %collective-permute-start.1 = (bf16[24,7168]{1,0:T(8,128)(2,1)S(1)}, bf16[24,7168]{1,0:T(8,128)(2,1)S(1)}, u32[]{:S(2)}, u32[]{:S(2)}) collective-permute-start(bf16[24,7168]{1,0:T(8,128)(2,1)S(1)} %fusion.1), channel_id=1, source_target_pairs={{0,64},{32,96},{1,65},{33,97},{2,66},{34,98},{3,67},{35,99},{4,68}... | collective-permute-start | bytes 1032200 | tf_op jit(solution)/shard_map/ppermute | solution.py:15
  223.1 7.9 %collective-permute-start.2 = (bf16[24,7168]{1,0:T(8,128)(2,1)S(1)}, bf16[24,7168]{1,0:T(8,128)(2,1)S(1)}, u32[]{:S(2)}, u32[]{:S(2)}) collective-permute-start(bf16[24,7168]{1,0:T(8,128)(2,1)S(1)} %fusion.1), channel_id=1, source_target_pairs={{0,32},{32,64},{64,96},{1,33},{33,65},{65,97},{2,34},{34,66},{66,9... | collective-permute-start | bytes 1032200 | tf_op jit(solution)/shard_map/ppermute | solution.py:15
  554.2 10.6 %collective-permute-start.3 = (bf16[32,6,7168]{2,0,1:T(8,128)(2,1)}, bf16[32,6,7168]{2,0,1:T(8,128)(2,1)S(1)}, u32[]{:S(2)}, u32[]{:S(2)}) collective-permute-start(bf16[32,6,7168]{2,0,1:T(8,128)(2,1)} %copy.54), channel_id=1, source_target_pairs={{32,0},{64,32},{96,64},{33,1},{65,33},{97,65},{34,2},{66,34},{98,6... | collective-permute-start | bytes 8257544 | tf_op jit(solution)/shard_map/ppermute | solution.py:15
  558.8 5.9 copy-start.6
  558.8 111.5 %collective-permute-start.4 = (bf16[32,6,7168]{2,0,1:T(8,128)(2,1)}, bf16[32,6,7168]{2,0,1:T(8,128)(2,1)}, u32[]{:S(2)}, u32[]{:S(2)}) collective-permute-start(bf16[32,6,7168]{2,0,1:T(8,128)(2,1)} %copy.55), channel_id=1, source_target_pairs={{64,0},{96,32},{65,1},{97,33},{66,2},{98,34},{67,3},{99,35},{68,4}... | collective-permute-start | bytes 8257544 | tf_op jit(solution)/shard_map/ppermute | solution.py:15
  563.4 113.9 %collective-permute-start.5 = (bf16[32,6,7168]{2,0,1:T(8,128)(2,1)}, bf16[32,6,7168]{2,0,1:T(8,128)(2,1)}, u32[]{:S(2)}, u32[]{:S(2)}) collective-permute-start(bf16[32,6,7168]{2,0,1:T(8,128)(2,1)} %copy.56), channel_id=1, source_target_pairs={{96,0},{97,1},{98,2},{99,3},{100,4},{101,5},{102,6},{103,7},{104,8... | collective-permute-start | bytes 8257544 | tf_op jit(solution)/shard_map/ppermute | solution.py:15
  677.4 7.0 %copy-start.1 = (bf16[8,64,576]{2,1,0:T(8,128)(2,1)S(1)}, bf16[8,64,576]{2,1,0:T(8,128)(2,1)}, u32[]{:S(2)}) copy-start(bf16[8,64,576]{2,1,0:T(8,128)(2,1)} %param.12) | copy-start | bytes 1769476
Sparse Core Ops, SparseCore 0:
  46.2 169.3 reduce-scatter.1
